TPU v7x, 256 devices: a whole 4x4x8 slice. The times are simulated.
256 devices in a mesh: clip: 8 (over x, core), frame: 32 (over y, z).
Axes of the slice: x: 4, y: 4, z: 8, core: 2. Of those that a mesh axis runs over, the one named last changes fastest.
Arguments:
- queries: bfloat16 [65536, 1024], P(('clip', 'frame')), may hold values from -216 to 216
- keys: bfloat16 [65536, 1024], P(('clip', 'frame')), may hold values from -6 to 6
- values: bfloat16 [65536, 1024], P(('clip', 'frame')), may hold values from -6 to 6
- cotangent: bfloat16 [65536, 1024], P(('clip', 'frame')), may hold values from -6 to 6
- partners: int32 [256, 6], P(('clip', 'frame')), may hold values from 0 to 255, as said below
- counts: int32 [256], P(('clip', 'frame')), may hold values from 1 to 6, as said below
Outputs:
- attended: bfloat16 [65536, 1024], P(('clip', 'frame'))
- query_grad: bfloat16 [65536, 1024], P(('clip', 'frame'))
- key_grad: bfloat16 [65536, 1024], P(('clip', 'frame'))
- value_grad: bfloat16 [65536, 1024], P(('clip', 'frame'))
Inputs may be any that keep to these rules, and one draw needn't show every extreme that they name: `partners`: row g lists distinct frames other than g, each either in g's clip group at most 2 positions away from g, or at g's position in the next or the previous clip group (cyclically). Entries past counts[g] are other frame ids. `counts`: some frame has all 6 entries live.
All inputs are finite; a program needn't handle non-finite values.
Results may differ from a plain program's by a relative error of at most 0.035.
Values may be sent and summed in bfloat16 or wider, within the bound.
A program may use at most 128 MiB of HBM per device.

v0:
```python
import functools
import math

import jax
import jax.numpy as jnp
from jax import lax
from jax.experimental import pallas as pl
from jax.experimental.pallas import tpu as pltpu
from jax.sharding import PartitionSpec as P

HEADS = 16
HEAD_DIM = 64
TOK = 256
WIDTH = 1024
SLOTS = 6
PAIR = 2 * HEAD_DIM
PAIRS = WIDTH // PAIR
SCALE = 1.0 / math.sqrt(HEAD_DIM)
FAR = 3e38
LAG = 3
MESH = pl.DeviceIdType.MESH

OWN = 6
FRAMES = 7


def kernel(
    partners, counts, q_hbm, k_hbm, v_hbm, g_hbm,
    att_hbm, dq_hbm, dk_hbm, dv_hbm,
    kv, tout, tin, pb, ds, q_in, g_in, qm, qt, gm, gt, o_t, dq_t, att_out, dq_out,
    mst, lst, cst, bias,
    in_sem, out_sem, kv_send, kv_recv, t_send, t_recv,
):
    c = lax.axis_index("clip")
    f = lax.axis_index("frame")
    clips = lax.axis_size("clip")
    frames = lax.axis_size("frame")
    right, left = (c, f + 1), (c, f - 1)
    up = (lax.rem(c + 1, clips), f)
    down = (lax.rem(c + clips - 1, clips), f)
    has_r, has_l = f < frames - 1, f > 0
    has_rr, has_ll = f < frames - 2, f > 1
    has_both = has_r & has_l

    def columns(p):
        return pl.ds(pl.multiple_of(p * PAIR, PAIR), PAIR)

    def fetch(i, p):
        src = (k_hbm, v_hbm, q_hbm, g_hbm)[i]
        dst = kv.at[OWN, p, i] if i < 2 else (q_in, g_in)[i - 2].at[p]
        return pltpu.make_async_copy(src.at[:, columns(p)], dst, in_sem.at[i, p])

    def store(i, p):
        src = (att_out, dq_out)[i].at[p] if i < 2 else tout.at[OWN, p, i - 2]
        dst = (att_hbm, dq_hbm, dk_hbm, dv_hbm)[i]
        return pltpu.make_async_copy(src, dst.at[:, columns(p)], out_sem.at[i, p])

    def remote(src, dst, send, recv, device):
        return pltpu.make_async_remote_copy(
            src_ref=src, dst_ref=dst, send_sem=send, recv_sem=recv, device_id=device, device_id_type=MESH
        )

    kv_routes = [
        (OWN, 5, right, has_r, has_l),
        (OWN, 4, left, has_l, has_r),
        (OWN, 3, up, None, None),
        (OWN, 2, down, None, None),
        (5, 1, right, has_both, has_ll),
        (4, 0, left, has_both, has_rr),
    ]

    def kv_copy(i, p):
        here, there, device, _, _ = kv_routes[i]
        return remote(kv.at[here, p], kv.at[there, p], kv_send.at[i, p], kv_recv.at[there, p], device)

    t_routes = [
        (0, 0, right, has_rr, has_both),
        (1, 1, left, has_ll, has_both),
        (2, 3, up, None, None),
        (3, 2, down, None, None),
        (4, 5, right, has_r, has_l),
        (5, 4, left, has_l, has_r),
    ]

    def t_copy(i, p):
        slot, there, device, _, _ = t_routes[i]
        return remote(tout.at[slot, p], tin.at[there, p], t_send.at[i, p], t_recv.at[there, p], device)

    def when(condition, action):
        if condition is None:
            action()
        else:
            pl.when(condition)(action)

    def start(copy, routes, i, p):
        when(routes[i][3], lambda: copy(i, p).start())

    def wait_send(copy, routes, i, p):
        when(routes[i][3], lambda: copy(i, p).wait_send())

    def wait_recv(copy, routes, i, p):
        when(routes[i][4], lambda: copy(i, p).wait_recv())

    def each_pair(body):
        def step(p, carry):
            body(p)
            return carry

        lax.fori_loop(0, PAIRS, step, 0)

    @each_pair
    def _(p):
        for i in range(4):
            fetch(i, p).start()

    barrier = pltpu.get_barrier_semaphore()
    for device, present in ((right, has_r), (left, has_l), (up, None), (down, None)):
        when(
            present,
            functools.partial(pl.semaphore_signal, barrier, inc=1, device_id=device, device_id_type=MESH),
        )
    pl.semaphore_wait(barrier, 2 + has_r.astype(jnp.int32) + has_l.astype(jnp.int32))

    @each_pair
    def _(p):
        for i in (0, 1):
            fetch(i, p).wait()
        for i in range(4):
            start(kv_copy, kv_routes, i, p)

    live = counts[0]
    me = c * frames + f
    targets = [
        (me + 2, has_rr),
        (me - 2, has_ll),
        (up[0] * frames + f, None),
        (down[0] * frames + f, None),
        (me + 1, has_r),
        (me - 1, has_l),
    ]
    for slot, (target, present) in enumerate(targets):
        found = jnp.int32(0)
        for s in range(SLOTS):
            found = found + jnp.where((partners[0, s] == target) & (s < live), 1, 0)
        if present is not None:
            found = jnp.where(present, found, 0)
        bias[slot] = jnp.where(found > 0, 0.0, FAR).astype(jnp.float32)
    bias[OWN] = jnp.float32(0.0)

    for slot, present in ((0, has_rr), (1, has_ll), (4, has_r), (5, has_l)):

        @pl.when(jnp.logical_not(present))
        def _():
            @each_pair
            def _(p):
                kv[slot, p] = jnp.zeros(kv.shape[2:], kv.dtype)

    for slot, present in ((0, has_both), (1, has_both), (4, has_r), (5, has_l)):

        @pl.when(jnp.logical_not(present))
        def _():
            @each_pair
            def _(p):
                tin[slot, p] = jnp.zeros(tin.shape[2:], tin.dtype)

    @each_pair
    def _(p):
        for i in (2, 3):
            fetch(i, p).wait()
        lane = lax.broadcasted_iota(jnp.int32, (TOK, PAIR), 1)
        row = lax.broadcasted_iota(jnp.int32, (PAIR, TOK), 0)
        q = q_in[p].astype(jnp.float32) * SCALE
        g = g_in[p].astype(jnp.float32)
        q_turned, g_turned = q.T, g.T
        for h in range(2):
            mine = (lane < HEAD_DIM) if h == 0 else (lane >= HEAD_DIM)
            mine_t = (row < HEAD_DIM) if h == 0 else (row >= HEAD_DIM)
            rows = pl.ds(h * TOK, TOK)
            qm[p, rows, :] = jnp.where(mine, q, 0.0).astype(jnp.bfloat16)
            gm[p, rows, :] = jnp.where(mine, g, 0.0).astype(jnp.bfloat16)
            qt[p, h] = jnp.where(mine_t, q_turned, 0.0).astype(jnp.bfloat16)
            gt[p, h] = jnp.where(mine_t, g_turned, 0.0).astype(jnp.bfloat16)

    def weigh(p, j):
        shift = bias[j]
        for h in range(2):
            cols = pl.ds(h * TOK, TOK)
            s = jnp.dot(kv[j, p, 0], qt[p, h], preferred_element_type=jnp.float32)
            top = jnp.max(s, axis=0, keepdims=True)
            e = jnp.exp(s - (top + shift))
            mst[p, j, :, cols] = top - shift
            lst[p, j, :, cols] = jnp.sum(e, axis=0, keepdims=True)
            pb[p, j, :, cols] = e.astype(jnp.bfloat16)

    def weigh_slots(p, first, last):
        def step(j, carry):
            weigh(p, j)
            return carry

        lax.fori_loop(first, last, step, 0)

    @each_pair
    def _(p):
        for i in (0, 1):
            wait_recv(kv_copy, kv_routes, i, p)
            start(kv_copy, kv_routes, 4 + i, p)
        for i in (2, 3):
            wait_recv(kv_copy, kv_routes, i, p)
        weigh_slots(p, 2, FRAMES)

    def near_terms(p):
        for i in (0, 1):
            wait_recv(t_copy, t_routes, i, p)
            total = tout[4 + i, p].astype(jnp.float32) + tin[i, p].astype(jnp.float32)
            tout[4 + i, p] = total.astype(jnp.bfloat16)
            start(t_copy, t_routes, 4 + i, p)

    @each_pair
    def _(p):
        for i in (4, 5):
            wait_recv(kv_copy, kv_routes, i, p)
        weigh_slots(p, 0, 2)

        top = jnp.max(mst[p], axis=0)
        total = jnp.zeros((1, 2 * TOK), jnp.float32)
        for j in range(FRAMES):
            e = jnp.exp(mst[p, j] - top)
            cst[j] = e
            total = total + e * lst[p, j]
        inverse = 1.0 / total
        for j in range(FRAMES):
            cst[j] = cst[j] * inverse

        o_t[...] = jnp.zeros_like(o_t)
        dq_t[...] = jnp.zeros_like(dq_t)

        def mix(j, carry):
            v_turned = kv[j, p, 1].T
            for h in range(2):
                cols = pl.ds(h * TOK, TOK)
                rows = slice(h * HEAD_DIM, (h + 1) * HEAD_DIM)
                part = jnp.dot(v_turned[rows], pb[p, j, :, cols], preferred_element_type=jnp.float32)
                o_t[rows] += part * cst[j, :, cols]
            return carry

        lax.fori_loop(0, FRAMES, mix, 0)
        attended = o_t[...].astype(jnp.bfloat16)
        attended_f = attended.astype(jnp.float32)
        att_out[p] = attended_f.T.astype(jnp.bfloat16)
        spread = [jnp.sum(gt[p, h].astype(jnp.float32) * attended_f, axis=0, keepdims=True) for h in range(2)]

        def grads(j, carry):
            k_turned = kv[j, p, 0].T
            for h in range(2):
                cols = pl.ds(h * TOK, TOK)
                rows = slice(h * HEAD_DIM, (h + 1) * HEAD_DIM)
                w = pb[p, j, :, cols].astype(jnp.float32) * cst[j, :, cols]
                pb[p, j, :, cols] = w.astype(jnp.bfloat16)
                dw = jnp.dot(kv[j, p, 1], gt[p, h], preferred_element_type=jnp.float32)
                d = (w * (dw - spread[h])).astype(jnp.bfloat16)
                ds[:, cols] = d
                dq_t[rows] += jnp.dot(k_turned[rows], d, preferred_element_type=jnp.float32)
            tout[j, p, 0] = jnp.dot(ds[...], qm[p], preferred_element_type=jnp.float32).astype(jnp.bfloat16)
            tout[j, p, 1] = jnp.dot(pb[p, j], gm[p], preferred_element_type=jnp.float32).astype(jnp.bfloat16)

            for after, sent in ((1, (0, 1)), (3, (2, 3))):

                @pl.when(j == after)
                def _():
                    for i in sent:
                        start(t_copy, t_routes, i, p)

            return carry

        lax.fori_loop(0, FRAMES, grads, 0)
        dq_out[p] = (dq_t[...] * SCALE).T.astype(jnp.bfloat16)
        for i in (0, 1):
            store(i, p).start()

        @pl.when(p >= LAG)
        def _():
            near_terms(p - LAG)

    def flush(p, carry):
        near_terms(p)
        return carry

    lax.fori_loop(PAIRS - LAG, PAIRS, flush, 0)

    @each_pair
    def _(p):
        for i in range(2, 6):
            wait_recv(t_copy, t_routes, i, p)
        total = tout[OWN, p].astype(jnp.float32)
        for i in range(2, 6):
            total = total + tin[i, p].astype(jnp.float32)
        tout[OWN, p] = total.astype(jnp.bfloat16)
        for i in (2, 3):
            store(i, p).start()

    @each_pair
    def _(p):
        for i in range(6):
            wait_send(kv_copy, kv_routes, i, p)
            wait_send(t_copy, t_routes, i, p)
        for i in range(4):
            store(i, p).wait()


def shards(queries, keys, values, cotangent, partners, counts):
    block = jax.ShapeDtypeStruct((TOK, WIDTH), jnp.bfloat16)
    smem = pl.BlockSpec(memory_space=pltpu.SMEM)
    whole = pl.BlockSpec(memory_space=pl.ANY)
    low = jnp.bfloat16
    return pl.pallas_call(
        kernel,
        out_shape=(block,) * 4,
        in_specs=[smem, smem] + [whole] * 4,
        out_specs=(whole,) * 4,
        scratch_shapes=[
            pltpu.VMEM((FRAMES, PAIRS, 2, TOK, PAIR), low),
            pltpu.VMEM((FRAMES, PAIRS, 2, TOK, PAIR), low),
            pltpu.VMEM((6, PAIRS, 2, TOK, PAIR), low),
            pltpu.VMEM((PAIRS, FRAMES, TOK, 2 * TOK), low),
            pltpu.VMEM((TOK, 2 * TOK), low),
            pltpu.VMEM((PAIRS, TOK, PAIR), low),
            pltpu.VMEM((PAIRS, TOK, PAIR), low),
            pltpu.VMEM((PAIRS, 2 * TOK, PAIR), low),
            pltpu.VMEM((PAIRS, 2, PAIR, TOK), low),
            pltpu.VMEM((PAIRS, 2 * TOK, PAIR), low),
            pltpu.VMEM((PAIRS, 2, PAIR, TOK), low),
            pltpu.VMEM((PAIR, TOK), jnp.float32),
            pltpu.VMEM((PAIR, TOK), jnp.float32),
            pltpu.VMEM((PAIRS, TOK, PAIR), low),
            pltpu.VMEM((PAIRS, TOK, PAIR), low),
            pltpu.VMEM((PAIRS, FRAMES, 1, 2 * TOK), jnp.float32),
            pltpu.VMEM((PAIRS, FRAMES, 1, 2 * TOK), jnp.float32),
            pltpu.VMEM((FRAMES, 1, 2 * TOK), jnp.float32),
            pltpu.SMEM((FRAMES,), jnp.float32),
            pltpu.SemaphoreType.DMA((4, PAIRS)),
            pltpu.SemaphoreType.DMA((4, PAIRS)),
            pltpu.SemaphoreType.DMA((6, PAIRS)),
            pltpu.SemaphoreType.DMA((6, PAIRS)),
            pltpu.SemaphoreType.DMA((6, PAIRS)),
            pltpu.SemaphoreType.DMA((6, PAIRS)),
        ],
        compiler_params=pltpu.CompilerParams(
            collective_id=0, has_side_effects=True, vmem_limit_bytes=60 * 2**20
        ),
    )(partners, counts, queries, keys, values, cotangent)


def solution(mesh):
    rows = P(("clip", "frame"), None)
    return jax.shard_map(
        shards,
        mesh=mesh,
        in_specs=(rows, rows, rows, rows, rows, P(("clip", "frame"))),
        out_specs=(rows, rows, rows, rows),
        check_vma=False,
    )
```

profile of v0, /device:TPU:30, one launch (start us, length us, event | category | flops | bytes accessed | tf_op | source)
XLA Modules:
  0.0 116.6 jit_solution(13037159260394494729)
XLA Ops:
  1.3 110.1 %shard_map.93 = (bf16[256,1024]{1,0:T(8,128)(2,1)}, bf16[256,1024]{1,0:T(8,128)(2,1)}, bf16[256,1024]{1,0:T(8,128)(2,1)}, bf16[256,1024]{1,0:T(8,128)(2,1)}) custom-call(s32[1,6]{1,0:T(1,128)} %partners.1, s32[1]{0:T(128)S(6)} %copy.14.counts, bf16[256,1024]{1,0:T(8,128)(2,1)} %q_hbm.1, bf16[256,1024]{1,0:T(8,128)(2,1)} %k_hbm.1, bf16[256,1024]{1,0:T(8,128)(2,1)} %v_hbm.1, ...), custom_call_target="tpu_custom_call" | custom-call | tf_op jit(solution)/shard_map/pallas_call | solution.py:315
  111.4 0.0 copy-start.2
  111.4 1.9 %copy.15 = bf16[256,1024]{1,0:T(8,128)(2,1)} copy(bf16[256,1024]{1,0:T(8,128)(2,1)} %get-tuple-element.8) | data formatting | bytes 1048576
  113.4 0.0 copy-done.2
  113.4 0.0 copy-start.1
  113.4 0.8 copy.16
  114.2 0.4 copy-done.1
  114.6 0.0 copy-start
  114.6 0.8 copy.17
  115.4 0.4 copy-done
  115.8 0.8 copy.18
Async XLA Ops:
  111.4 1.9 %copy-start.2 = (bf16[256,1024]{1,0:T(8,128)(2,1)S(1)}, bf16[256,1024]{1,0:T(8,128)(2,1)}, u32[]{:S(2)}) copy-start(bf16[256,1024]{1,0:T(8,128)(2,1)} %get-tuple-element.9) | copy-start | bytes 1572868
  113.4 1.2 %copy-start.1 = (bf16[256,1024]{1,0:T(8,128)(2,1)S(1)}, bf16[256,1024]{1,0:T(8,128)(2,1)}, u32[]{:S(2)}) copy-start(bf16[256,1024]{1,0:T(8,128)(2,1)} %get-tuple-element.10) | copy-start | bytes 1572868
  114.6 1.2 %copy-start = (bf16[256,1024]{1,0:T(8,128)(2,1)S(1)}, bf16[256,1024]{1,0:T(8,128)(2,1)}, u32[]{:S(2)}) copy-start(bf16[256,1024]{1,0:T(8,128)(2,1)} %get-tuple-element.11) | copy-start | bytes 1572868
where the time goes:
time: 117 us
  Pallas kernels  110 us (94%)
  local copies, waits for them, and re-layouts  5.18 us (4%)
  between operations  1.3 us (1%)
    pallas_call x1, Pallas kernels, shards(): pl.pallas_call(kernel, out_shape=(block,) * 4, in_specs=[smem, smem] + [w...  110 us
    unnamed x10, local copies, waits for them, and re-layouts  5.18 us

commit v1 on v0

--- a/solution.py
+++ b/solution.py
@@ -22,13 +22,14 @@
 
 OWN = 6
 FRAMES = 7
+EARLY = (6, 2, 3, 4, 5)
 
 
 def kernel(
-    partners, counts, q_hbm, k_hbm, v_hbm, g_hbm,
+    partners_hbm, counts_hbm, q_hbm, k_hbm, v_hbm, g_hbm,
     att_hbm, dq_hbm, dk_hbm, dv_hbm,
-    kv, tout, tin, pb, ds, q_in, g_in, qm, qt, gm, gt, o_t, dq_t, att_out, dq_out,
-    mst, lst, cst, bias,
+    kv, tout, tin, pb, q_in, g_in, qm, qt, gm, gt, o_t, att_out, dq_out,
+    mst, lst, bias, partners, counts, list_sem,
     in_sem, out_sem, kv_send, kv_recv, t_send, t_recv,
 ):
     c = lax.axis_index("clip")
@@ -108,6 +109,13 @@
 
         lax.fori_loop(0, PAIRS, step, 0)
 
+    lists = [
+        pltpu.make_async_copy(partners_hbm, partners, list_sem.at[0]),
+        pltpu.make_async_copy(counts_hbm, counts, list_sem.at[1]),
+    ]
+    for copy in lists:
+        copy.start()
+
     @each_pair
     def _(p):
         for i in range(4):
@@ -128,6 +136,8 @@
         for i in range(4):
             start(kv_copy, kv_routes, i, p)
 
+    for copy in lists:
+        copy.wait()
     live = counts[0]
     me = c * frames + f
     targets = [
@@ -181,23 +191,43 @@
             qt[p, h] = jnp.where(mine_t, q_turned, 0.0).astype(jnp.bfloat16)
             gt[p, h] = jnp.where(mine_t, g_turned, 0.0).astype(jnp.bfloat16)
 
-    def weigh(p, j):
-        shift = bias[j]
-        for h in range(2):
-            cols = pl.ds(h * TOK, TOK)
-            s = jnp.dot(kv[j, p, 0], qt[p, h], preferred_element_type=jnp.float32)
-            top = jnp.max(s, axis=0, keepdims=True)
-            e = jnp.exp(s - (top + shift))
-            mst[p, j, :, cols] = top - shift
-            lst[p, j, :, cols] = jnp.sum(e, axis=0, keepdims=True)
-            pb[p, j, :, cols] = e.astype(jnp.bfloat16)
-
-    def weigh_slots(p, first, last):
-        def step(j, carry):
-            weigh(p, j)
-            return carry
-
-        lax.fori_loop(first, last, step, 0)
+    halves = [slice(h * HEAD_DIM, (h + 1) * HEAD_DIM) for h in range(2)]
+    both = [slice(h * TOK, (h + 1) * TOK) for h in range(2)]
+
+    def mul(a, b):
+        return jnp.dot(a, b, preferred_element_type=jnp.float32)
+
+    def weigh(p, slots):
+        def front(j):
+            return [mul(kv[j, p, 0], qt[p, h]) for h in range(2)]
+
+        def middle(j, scores):
+            tops, sums = [], []
+            for h in range(2):
+                top = jnp.max(scores[h], axis=0, keepdims=True)
+                e = jnp.exp(scores[h] - (top + bias[j]))
+                tops.append(top - bias[j])
+                sums.append(jnp.sum(e, axis=0, keepdims=True))
+                pb[p, j, :, both[h]] = e.astype(jnp.bfloat16)
+            return jnp.concatenate(tops, axis=1), jnp.concatenate(sums, axis=1)
+
+        def back(j):
+            v_turned = kv[j, p, 1].T
+            return [mul(v_turned[halves[h]], pb[p, j, :, both[h]]) for h in range(2)]
+
+        coming = front(slots[0])
+        tops, sums, parts = [], [], []
+        for n, j in enumerate(slots):
+            scores = coming
+            if n + 1 < len(slots):
+                coming = front(slots[n + 1])
+            if n > 0:
+                parts.append(back(slots[n - 1]))
+            top, total = middle(j, scores)
+            tops.append(top)
+            sums.append(total)
+        parts.append(back(slots[-1]))
+        return tops, sums, parts
 
     @each_pair
     def _(p):
@@ -206,7 +236,19 @@
             start(kv_copy, kv_routes, 4 + i, p)
         for i in (2, 3):
             wait_recv(kv_copy, kv_routes, i, p)
-        weigh_slots(p, 2, FRAMES)
+        tops, sums, parts = weigh(p, EARLY)
+        top = functools.reduce(jnp.maximum, tops)
+        total = jnp.zeros_like(top)
+        mixed = [jnp.zeros((HEAD_DIM, TOK), jnp.float32) for _ in range(2)]
+        for n, j in enumerate(EARLY):
+            e = jnp.exp(tops[n] - top)
+            mst[p, j] = tops[n]
+            total = total + e * sums[n]
+            mixed = [mixed[h] + parts[n][h] * e[:, both[h]] for h in range(2)]
+        mst[p, FRAMES] = top
+        lst[p] = total
+        for h in range(2):
+            o_t[p, halves[h]] = mixed[h]
 
     def near_terms(p):
         for i in (0, 1):
@@ -219,61 +261,57 @@
     def _(p):
         for i in (4, 5):
             wait_recv(kv_copy, kv_routes, i, p)
-        weigh_slots(p, 0, 2)
-
-        top = jnp.max(mst[p], axis=0)
-        total = jnp.zeros((1, 2 * TOK), jnp.float32)
-        for j in range(FRAMES):
-            e = jnp.exp(mst[p, j] - top)
-            cst[j] = e
-            total = total + e * lst[p, j]
-        inverse = 1.0 / total
-        for j in range(FRAMES):
-            cst[j] = cst[j] * inverse
-
-        o_t[...] = jnp.zeros_like(o_t)
-        dq_t[...] = jnp.zeros_like(dq_t)
-
-        def mix(j, carry):
-            v_turned = kv[j, p, 1].T
+        tops, sums, parts = weigh(p, (0, 1))
+        tops = tops + [mst[p, j] for j in range(2, FRAMES)]
+        early = mst[p, FRAMES]
+        top = functools.reduce(jnp.maximum, [tops[0], tops[1], early])
+        factors = [jnp.exp(t - top) for t in tops]
+        early = jnp.exp(early - top)
+        inverse = 1.0 / (early * lst[p] + factors[0] * sums[0] + factors[1] * sums[1])
+        factors = [e * inverse for e in factors]
+        early = early * inverse
+
+        g_turned = gt[p, 0] + gt[p, 1]
+        spread, attended = [], []
+        for h in range(2):
+            total = o_t[p, halves[h]] * early[:, both[h]]
+            for j in (0, 1):
+                total = total + parts[j][h] * factors[j][:, both[h]]
+            total = total.astype(jnp.bfloat16).astype(jnp.float32)
+            attended.append(total)
+            spread.append(jnp.sum(g_turned[halves[h]].astype(jnp.float32) * total, axis=0, keepdims=True))
+        att_out[p] = jnp.concatenate(attended, axis=0).T.astype(jnp.bfloat16)
+
+        dq_parts = [jnp.zeros((HEAD_DIM, TOK), jnp.float32) for _ in range(2)]
+
+        def front(j):
+            return [mul(kv[j, p, 1], gt[p, h]) for h in range(2)]
+
+        def middle(j, dws):
+            ws, dss = [], []
             for h in range(2):
-                cols = pl.ds(h * TOK, TOK)
-                rows = slice(h * HEAD_DIM, (h + 1) * HEAD_DIM)
-                part = jnp.dot(v_turned[rows], pb[p, j, :, cols], preferred_element_type=jnp.float32)
-                o_t[rows] += part * cst[j, :, cols]
-            return carry
-
-        lax.fori_loop(0, FRAMES, mix, 0)
-        attended = o_t[...].astype(jnp.bfloat16)
-        attended_f = attended.astype(jnp.float32)
-        att_out[p] = attended_f.T.astype(jnp.bfloat16)
-        spread = [jnp.sum(gt[p, h].astype(jnp.float32) * attended_f, axis=0, keepdims=True) for h in range(2)]
-
-        def grads(j, carry):
+                w = pb[p, j, :, both[h]].astype(jnp.float32) * factors[j][:, both[h]]
+                ws.append(w.astype(jnp.bfloat16))
+                dss.append((w * (dws[h] - spread[h])).astype(jnp.bfloat16))
+            return jnp.concatenate(ws, axis=1), jnp.concatenate(dss, axis=1)
+
+        def back(j, ws, dss):
+            tout[j, p, 1] = mul(ws, gm[p]).astype(jnp.bfloat16)
+            tout[j, p, 0] = mul(dss, qm[p]).astype(jnp.bfloat16)
             k_turned = kv[j, p, 0].T
             for h in range(2):
-                cols = pl.ds(h * TOK, TOK)
-                rows = slice(h * HEAD_DIM, (h + 1) * HEAD_DIM)
-                w = pb[p, j, :, cols].astype(jnp.float32) * cst[j, :, cols]
-                pb[p, j, :, cols] = w.astype(jnp.bfloat16)
-                dw = jnp.dot(kv[j, p, 1], gt[p, h], preferred_element_type=jnp.float32)
-                d = (w * (dw - spread[h])).astype(jnp.bfloat16)
-                ds[:, cols] = d
-                dq_t[rows] += jnp.dot(k_turned[rows], d, preferred_element_type=jnp.float32)
-            tout[j, p, 0] = jnp.dot(ds[...], qm[p], preferred_element_type=jnp.float32).astype(jnp.bfloat16)
-            tout[j, p, 1] = jnp.dot(pb[p, j], gm[p], preferred_element_type=jnp.float32).astype(jnp.bfloat16)
-
-            for after, sent in ((1, (0, 1)), (3, (2, 3))):
-
-                @pl.when(j == after)
-                def _():
-                    for i in sent:
-                        start(t_copy, t_routes, i, p)
-
-            return carry
-
-        lax.fori_loop(0, FRAMES, grads, 0)
-        dq_out[p] = (dq_t[...] * SCALE).T.astype(jnp.bfloat16)
+                dq_parts[h] = dq_parts[h] + mul(k_turned[halves[h]], dss[:, both[h]])
+
+        ready = middle(0, front(0))
+        for j in range(FRAMES):
+            coming = front(j + 1) if j + 1 < FRAMES else None
+            back(j, *ready)
+            if j + 1 < FRAMES:
+                ready = middle(j + 1, coming)
+
+        for i in range(4):
+            start(t_copy, t_routes, i, p)
+        dq_out[p] = (jnp.concatenate(dq_parts, axis=0) * SCALE).T.astype(jnp.bfloat16)
         for i in (0, 1):
             store(i, p).start()
 
@@ -307,36 +345,48 @@
             store(i, p).wait()
 
 
+def hand_over(*refs):
+    sources, targets, (held, sem) = refs[:4], refs[4:8], refs[8:]
+    come = [pltpu.make_async_copy(sources[i], held.at[i], sem.at[0, i]) for i in range(4)]
+    go = [pltpu.make_async_copy(held.at[i], targets[i], sem.at[1, i]) for i in range(4)]
+    for copy in come:
+        copy.start()
+    for i in range(4):
+        come[i].wait()
+        go[i].start()
+    for copy in go:
+        copy.wait()
+
+
 def shards(queries, keys, values, cotangent, partners, counts):
     block = jax.ShapeDtypeStruct((TOK, WIDTH), jnp.bfloat16)
-    smem = pl.BlockSpec(memory_space=pltpu.SMEM)
     whole = pl.BlockSpec(memory_space=pl.ANY)
     low = jnp.bfloat16
-    return pl.pallas_call(
+    results = pl.pallas_call(
         kernel,
         out_shape=(block,) * 4,
-        in_specs=[smem, smem] + [whole] * 4,
+        in_specs=[whole] * 6,
         out_specs=(whole,) * 4,
         scratch_shapes=[
             pltpu.VMEM((FRAMES, PAIRS, 2, TOK, PAIR), low),
             pltpu.VMEM((FRAMES, PAIRS, 2, TOK, PAIR), low),
             pltpu.VMEM((6, PAIRS, 2, TOK, PAIR), low),
             pltpu.VMEM((PAIRS, FRAMES, TOK, 2 * TOK), low),
-            pltpu.VMEM((TOK, 2 * TOK), low),
             pltpu.VMEM((PAIRS, TOK, PAIR), low),
             pltpu.VMEM((PAIRS, TOK, PAIR), low),
             pltpu.VMEM((PAIRS, 2 * TOK, PAIR), low),
             pltpu.VMEM((PAIRS, 2, PAIR, TOK), low),
             pltpu.VMEM((PAIRS, 2 * TOK, PAIR), low),
             pltpu.VMEM((PAIRS, 2, PAIR, TOK), low),
-            pltpu.VMEM((PAIR, TOK), jnp.float32),
-            pltpu.VMEM((PAIR, TOK), jnp.float32),
+            pltpu.VMEM((PAIRS, PAIR, TOK), jnp.float32),
             pltpu.VMEM((PAIRS, TOK, PAIR), low),
             pltpu.VMEM((PAIRS, TOK, PAIR), low),
-            pltpu.VMEM((PAIRS, FRAMES, 1, 2 * TOK), jnp.float32),
-            pltpu.VMEM((PAIRS, FRAMES, 1, 2 * TOK), jnp.float32),
-            pltpu.VMEM((FRAMES, 1, 2 * TOK), jnp.float32),
+            pltpu.VMEM((PAIRS, FRAMES + 1, 1, 2 * TOK), jnp.float32),
+            pltpu.VMEM((PAIRS, 1, 2 * TOK), jnp.float32),
             pltpu.SMEM((FRAMES,), jnp.float32),
+            pltpu.SMEM((1, SLOTS), jnp.int32),
+            pltpu.SMEM((1,), jnp.int32),
+            pltpu.SemaphoreType.DMA((2,)),
             pltpu.SemaphoreType.DMA((4, PAIRS)),
             pltpu.SemaphoreType.DMA((4, PAIRS)),
             pltpu.SemaphoreType.DMA((6, PAIRS)),
@@ -348,6 +398,13 @@
             collective_id=0, has_side_effects=True, vmem_limit_bytes=60 * 2**20
         ),
     )(partners, counts, queries, keys, values, cotangent)
+    return pl.pallas_call(
+        hand_over,
+        out_shape=(block,) * 4,
+        in_specs=[whole] * 4,
+        out_specs=(whole,) * 4,
+        scratch_shapes=[pltpu.VMEM((4, TOK, WIDTH), low), pltpu.SemaphoreType.DMA((2, 4))],
+    )(*results)
 
 
 def solution(mesh):

time: 117 us -> 106 us (0.906); the launches traced: 117 us -> 104 us
  Pallas kernels: 110 us -> 103 us
  local copies, waits for them, and re-layouts: 5.18 us -> 0 us
    pallas_call x1 -> x2, Pallas kernels: 110 us -> 103 us  [the longest x1 101 us: shards(): pl.pallas_call(kernel, out_shape=(block,) * 4, in_specs=[whole] * 6, out_...]
    unnamed x10 -> x0, local copies, waits for them, and re-layouts: 5.18 us -> none
where the time goes in v1:
time: 106 us; the launch traced here: 104 us
  Pallas kernels  103 us (97%)
  between operations  1.29 us (1%)
    pallas_call x1, Pallas kernels, shards(): pl.pallas_call(kernel, out_shape=(block,) * 4, in_specs=[whole] * 6, out_...  101 us
    pallas_call x1, Pallas kernels, shards(): pl.pallas_call(hand_over, out_shape=(block,) * 4, in_specs=[whole] * 4, o...  2.42 us

profile of v1, /device:TPU:30, one launch (start us, length us, event | category | flops | bytes accessed | tf_op | source)
XLA Modules:
  0.0 104.4 jit_solution(16417764290139138707)
XLA Ops:
  1.3 100.7 %shard_map.93 = (bf16[256,1024]{1,0:T(8,128)(2,1)}, bf16[256,1024]{1,0:T(8,128)(2,1)}, bf16[256,1024]{1,0:T(8,128)(2,1)}, bf16[256,1024]{1,0:T(8,128)(2,1)}) custom-call(s32[1,6]{1,0:T(1,128)} %partners_hbm.1, s32[1]{0:T(128)S(6)} %copy.10.counts_hbm, bf16[256,1024]{1,0:T(8,128)(2,1)} %q_hbm.1, bf16[256,1024]{1,0:T(8,128)(2,1)} %k_hbm.1, ...), custom_call_target="tpu_custom_call" | custom-call | tf_op jit(solution)/shard_map/pallas_call | solution.py:365
  102.0 2.4 %shard_map.94 = (bf16[256,1024]{1,0:T(8,128)(2,1)}, bf16[256,1024]{1,0:T(8,128)(2,1)}, bf16[256,1024]{1,0:T(8,128)(2,1)}, bf16[256,1024]{1,0:T(8,128)(2,1)}) custom-call(bf16[256,1024]{1,0:T(8,128)(2,1)} %get-tuple-element.8.refs_0_, bf16[256,1024]{1,0:T(8,128)(2,1)} %get-tuple-element.9.refs_1_, bf16[256,1024]{1,0:T(8,128)(2,1)} %get-tuple-element.10.refs_2_, ...), custom_call_target="tpu_custom_call" | custom-call | tf_op jit(solution)/shard_map/pallas_call | solution.py:401

commit v2 on v1

--- a/solution.py
+++ b/solution.py
@@ -27,10 +27,10 @@
 
 def kernel(
     partners_hbm, counts_hbm, q_hbm, k_hbm, v_hbm, g_hbm,
-    att_hbm, dq_hbm, dk_hbm, dv_hbm,
-    kv, tout, tin, pb, q_in, g_in, qm, qt, gm, gt, o_t, att_out, dq_out,
+    att, dq, dk, dv,
+    kv, tout, tin, pb, q_in, g_in, qm, qt, gm, gt, o_t,
     mst, lst, bias, partners, counts, list_sem,
-    in_sem, out_sem, kv_send, kv_recv, t_send, t_recv,
+    in_sem, kv_send, kv_recv, t_send, t_recv,
 ):
     c = lax.axis_index("clip")
     f = lax.axis_index("frame")
@@ -51,11 +51,6 @@
         dst = kv.at[OWN, p, i] if i < 2 else (q_in, g_in)[i - 2].at[p]
         return pltpu.make_async_copy(src.at[:, columns(p)], dst, in_sem.at[i, p])
 
-    def store(i, p):
-        src = (att_out, dq_out)[i].at[p] if i < 2 else tout.at[OWN, p, i - 2]
-        dst = (att_hbm, dq_hbm, dk_hbm, dv_hbm)[i]
-        return pltpu.make_async_copy(src, dst.at[:, columns(p)], out_sem.at[i, p])
-
     def remote(src, dst, send, recv, device):
         return pltpu.make_async_remote_copy(
             src_ref=src, dst_ref=dst, send_sem=send, recv_sem=recv, device_id=device, device_id_type=MESH
@@ -138,7 +133,7 @@
 
     for copy in lists:
         copy.wait()
-    live = counts[0]
+    live = counts[0, 0]
     me = c * frames + f
     targets = [
         (me + 2, has_rr),
@@ -280,7 +275,7 @@
             total = total.astype(jnp.bfloat16).astype(jnp.float32)
             attended.append(total)
             spread.append(jnp.sum(g_turned[halves[h]].astype(jnp.float32) * total, axis=0, keepdims=True))
-        att_out[p] = jnp.concatenate(attended, axis=0).T.astype(jnp.bfloat16)
+        att[:, columns(p)] = jnp.concatenate(attended, axis=0).T.astype(jnp.bfloat16)
 
         dq_parts = [jnp.zeros((HEAD_DIM, TOK), jnp.float32) for _ in range(2)]
 
@@ -311,9 +306,7 @@
 
         for i in range(4):
             start(t_copy, t_routes, i, p)
-        dq_out[p] = (jnp.concatenate(dq_parts, axis=0) * SCALE).T.astype(jnp.bfloat16)
-        for i in (0, 1):
-            store(i, p).start()
+        dq[:, columns(p)] = (jnp.concatenate(dq_parts, axis=0) * SCALE).T.astype(jnp.bfloat16)
 
         @pl.when(p >= LAG)
         def _():
@@ -332,41 +325,36 @@
         total = tout[OWN, p].astype(jnp.float32)
         for i in range(2, 6):
             total = total + tin[i, p].astype(jnp.float32)
-        tout[OWN, p] = total.astype(jnp.bfloat16)
-        for i in (2, 3):
-            store(i, p).start()
+        dk[:, columns(p)] = total[0].astype(jnp.bfloat16)
+        dv[:, columns(p)] = total[1].astype(jnp.bfloat16)
 
     @each_pair
     def _(p):
         for i in range(6):
             wait_send(kv_copy, kv_routes, i, p)
             wait_send(t_copy, t_routes, i, p)
-        for i in range(4):
-            store(i, p).wait()
 
 
 def hand_over(*refs):
-    sources, targets, (held, sem) = refs[:4], refs[4:8], refs[8:]
-    come = [pltpu.make_async_copy(sources[i], held.at[i], sem.at[0, i]) for i in range(4)]
-    go = [pltpu.make_async_copy(held.at[i], targets[i], sem.at[1, i]) for i in range(4)]
-    for copy in come:
+    sem = refs[-1]
+    half = (len(refs) - 1) // 2
+    copies = [pltpu.make_async_copy(refs[i], refs[half + i], sem.at[i]) for i in range(half)]
+    for copy in copies:
         copy.start()
-    for i in range(4):
-        come[i].wait()
-        go[i].start()
-    for copy in go:
+    for copy in copies:
         copy.wait()
 
 
 def shards(queries, keys, values, cotangent, partners, counts):
     block = jax.ShapeDtypeStruct((TOK, WIDTH), jnp.bfloat16)
     whole = pl.BlockSpec(memory_space=pl.ANY)
+    near = pl.BlockSpec(memory_space=pltpu.VMEM)
     low = jnp.bfloat16
     results = pl.pallas_call(
         kernel,
-        out_shape=(block,) * 4,
+        out_shape=(pltpu.VMEM((TOK, WIDTH), low),) * 4,
         in_specs=[whole] * 6,
-        out_specs=(whole,) * 4,
+        out_specs=(near,) * 4,
         scratch_shapes=[
             pltpu.VMEM((FRAMES, PAIRS, 2, TOK, PAIR), low),
             pltpu.VMEM((FRAMES, PAIRS, 2, TOK, PAIR), low),
@@ -379,15 +367,12 @@
             pltpu.VMEM((PAIRS, 2 * TOK, PAIR), low),
             pltpu.VMEM((PAIRS, 2, PAIR, TOK), low),
             pltpu.VMEM((PAIRS, PAIR, TOK), jnp.float32),
-            pltpu.VMEM((PAIRS, TOK, PAIR), low),
-            pltpu.VMEM((PAIRS, TOK, PAIR), low),
             pltpu.VMEM((PAIRS, FRAMES + 1, 1, 2 * TOK), jnp.float32),
             pltpu.VMEM((PAIRS, 1, 2 * TOK), jnp.float32),
             pltpu.SMEM((FRAMES,), jnp.float32),
             pltpu.SMEM((1, SLOTS), jnp.int32),
-            pltpu.SMEM((1,), jnp.int32),
+            pltpu.SMEM((1, 1), jnp.int32),
             pltpu.SemaphoreType.DMA((2,)),
-            pltpu.SemaphoreType.DMA((4, PAIRS)),
             pltpu.SemaphoreType.DMA((4, PAIRS)),
             pltpu.SemaphoreType.DMA((6, PAIRS)),
             pltpu.SemaphoreType.DMA((6, PAIRS)),
@@ -395,16 +380,20 @@
             pltpu.SemaphoreType.DMA((6, PAIRS)),
         ],
         compiler_params=pltpu.CompilerParams(
-            collective_id=0, has_side_effects=True, vmem_limit_bytes=60 * 2**20
+            collective_id=0, has_side_effects=True, vmem_limit_bytes=48 * 2**20
         ),
-    )(partners, counts, queries, keys, values, cotangent)
+    )(
+        pltpu.with_memory_space_constraint(partners, pltpu.HBM),
+        counts.reshape(1, 1),
+        *[pltpu.with_memory_space_constraint(x, pltpu.HBM) for x in (queries, keys, values, cotangent)],
+    )
     return pl.pallas_call(
         hand_over,
         out_shape=(block,) * 4,
-        in_specs=[whole] * 4,
+        in_specs=[near] * 4,
         out_specs=(whole,) * 4,
-        scratch_shapes=[pltpu.VMEM((4, TOK, WIDTH), low), pltpu.SemaphoreType.DMA((2, 4))],
-    )(*results)
+        scratch_shapes=[pltpu.SemaphoreType.DMA((4,))],
+    )(*[pltpu.with_memory_space_constraint(x, pltpu.VMEM) for x in results])
 
 
 def solution(mesh):

time: 106 us -> 104 us (0.981)
  Pallas kernels: 103 us -> 101 us
    pallas_call x2, Pallas kernels: 103 us -> 101 us  [the longest x1 100 us: shards(): pl.pallas_call(kernel, out_shape=(pltpu.VMEM((TOK, WIDTH), low),) * 4, in...]
where the time goes in v2:
time: 104 us; the launch traced here: 103 us
  Pallas kernels  101 us (97%)
  between operations  1.29 us (1%)
    pallas_call x1, Pallas kernels, shards(): pl.pallas_call(kernel, out_shape=(pltpu.VMEM((TOK, WIDTH), low),) * 4, in...  100 us

profile of v2, /device:TPU:30, one launch (start us, length us, event | category | flops | bytes accessed | tf_op | source)
XLA Modules:
  0.0 102.6 jit_solution(17325430602892832047)
XLA Ops:
  1.3 100.0 %shard_map.93 = (bf16[256,1024]{1,0:T(8,128)(2,1)S(1)}, bf16[256,1024]{1,0:T(8,128)(2,1)S(1)}, bf16[256,1024]{1,0:T(8,128)(2,1)S(1)}, bf16[256,1024]{1,0:T(8,128)(2,1)S(1)}) custom-call(s32[1,6]{1,0:T(1,128)} %partners_hbm.1, s32[1,1]{1,0:T(1,128)} %bitcast.1.counts_hbm, bf16[256,1024]{1,0:T(8,128)(2,1)} %q_hbm.1, bf16[256,1024]{1,0:T(8,128)(2,1)} %k_hbm.1, ...), custom_call_target="tpu_custom_call" | custom-call | tf_op jit(solution)/shard_map/pallas_call | solution.py:353
  101.2 1.3 %shard_map.94 = (bf16[256,1024]{1,0:T(8,128)(2,1)}, bf16[256,1024]{1,0:T(8,128)(2,1)}, bf16[256,1024]{1,0:T(8,128)(2,1)}, bf16[256,1024]{1,0:T(8,128)(2,1)}) custom-call(bf16[256,1024]{1,0:T(8,128)(2,1)S(1)} %get-tuple-element.8.refs_0_, bf16[256,1024]{1,0:T(8,128)(2,1)S(1)} %get-tuple-element.9.refs_1_, bf16[256,1024]{1,0:T(8,128)(2,1)S(1)} %get-tuple-element.10.refs_2_, ...), custom_call_target="tpu_custom_call" | custom-call | tf_op jit(solution)/shard_map/pallas_call | solution.py:390

commit v3 on v2

--- a/solution.py
+++ b/solution.py
@@ -20,6 +20,13 @@
 LAG = 3
 MESH = pl.DeviceIdType.MESH
 
+SEAMS = ((7, 8), (15, 16), (23, 24))
+RELAYS = ((31, 23, 31), (0, 8, 0))
+DETOURS = ((2, 2, 4), (4, 2, 2))
+MOST = 4
+RELAY_AT = (2, 2, 3)
+HEADSTART = 2
+
 OWN = 6
 FRAMES = 7
 EARLY = (6, 2, 3, 4, 5)
@@ -31,6 +38,7 @@
     kv, tout, tin, pb, q_in, g_in, qm, qt, gm, gt, o_t,
     mst, lst, bias, partners, counts, list_sem,
     in_sem, kv_send, kv_recv, t_send, t_recv,
+    relayed, relay_send, relay_recv, seam_ok, relay_ok, far_ok,
 ):
     c = lax.axis_index("clip")
     f = lax.axis_index("frame")
@@ -43,6 +51,11 @@
     has_rr, has_ll = f < frames - 2, f > 1
     has_both = has_r & has_l
 
+    def is_any(*ids):
+        return functools.reduce(jnp.logical_or, [f == i for i in ids])
+
+    before, after = (is_any(*(seam[side] for seam in SEAMS)) for side in range(2))
+
     def columns(p):
         return pl.ds(pl.multiple_of(p * PAIR, PAIR), PAIR)
 
@@ -116,20 +129,91 @@
         for i in range(4):
             fetch(i, p).start()
 
+    def signal(semaphore, device):
+        pl.semaphore_signal(semaphore, inc=1, device_id=device, device_id_type=MESH)
+
+    def signal_frames(condition, *ids):
+        @pl.when(condition)
+        def _():
+            for i in ids:
+                signal(barrier, (c, i))
+
     barrier = pltpu.get_barrier_semaphore()
-    for device, present in ((right, has_r), (left, has_l), (up, None), (down, None)):
-        when(
-            present,
-            functools.partial(pl.semaphore_signal, barrier, inc=1, device_id=device, device_id_type=MESH),
-        )
-    pl.semaphore_wait(barrier, 2 + has_r.astype(jnp.int32) + has_l.astype(jnp.int32))
+    pl.when(has_r & jnp.logical_not(before))(lambda: signal(barrier, right))
+    pl.when(has_l)(lambda: signal(barrier, left))
+    signal(barrier, up)
+    signal(barrier, down)
+    signal_frames(is_any(7, 8, 23, 24), 0, 31)
+    signal_frames(f == 15, 23)
+    signal_frames(f == 16, 23, 8)
+    signal_frames(f == 8, 15)
+
+    def amount(condition, count):
+        return count * condition.astype(jnp.int32)
+
+    greeted = 2 + amount(has_r, 1) + amount(has_l & jnp.logical_not(after), 1)
+    greeted = greeted + amount(is_any(0, 31), 4) + amount(f == 23, 2) + amount(is_any(8, 15), 1)
+    pl.semaphore_wait(barrier, greeted)
+    pl.when(before)(lambda: signal(seam_ok, right))
+    pl.when(f == 15)(lambda: signal(far_ok, (c, 8)))
+    sides = [(side, k) for k in range(len(SEAMS)) for side in range(2)]
+    for side, k in sides:
+        pl.when(f == RELAYS[side][k])(lambda: signal(relay_ok, (c, SEAMS[k][side])))
+
+    def detour(side, k, n):
+        pair = PAIRS - DETOURS[side][k] + n
+        device = (c, RELAYS[side][k])
+        return remote(kv.at[OWN, pair], relayed.at[k, n], kv_send.at[side, pair], relay_recv.at[k, n], device)
+
+    def relay(side, k, n):
+        pair, slot = PAIRS - DETOURS[side][k] + n, 5 - side
+        device = (c, SEAMS[k][1 - side])
+        return remote(relayed.at[k, n], kv.at[slot, pair], relay_send.at[k, n], kv_recv.at[slot, pair], device)
 
     @each_pair
     def _(p):
         for i in (0, 1):
             fetch(i, p).wait()
-        for i in range(4):
-            start(kv_copy, kv_routes, i, p)
+
+    direct = [
+        PAIRS - sum(amount(f == seam[side], count) for seam, count in zip(SEAMS, DETOURS[side])) for side in range(2)
+    ]
+
+    def send_own(p, carry):
+        pl.when(has_r & (p < direct[0]))(lambda: kv_copy(0, p).start())
+        pl.when(has_l & (p < direct[1]) & jnp.logical_not(after & (p < HEADSTART)))(lambda: kv_copy(1, p).start())
+        for i in (2, 3):
+            kv_copy(i, p).start()
+        return carry
+
+    lax.fori_loop(0, HEADSTART, send_own, 0)
+
+    @pl.when(after)
+    def _():
+        pl.semaphore_wait(seam_ok, 1)
+        for p in range(HEADSTART):
+            kv_copy(1, p).start()
+
+    for side, k in sides:
+
+        @pl.when(f == SEAMS[k][side])
+        def _():
+            pl.semaphore_wait(relay_ok, 1)
+            for n in range(DETOURS[side][k]):
+                detour(side, k, n).start()
+
+    lax.fori_loop(HEADSTART, PAIRS, send_own, 0)
+
+    def pass_on(k):
+        for side in range(2):
+
+            @pl.when(f == RELAYS[side][k])
+            def _():
+                if RELAYS[side][k] == 8:
+                    pl.semaphore_wait(far_ok, 1)
+                for n in range(DETOURS[side][k]):
+                    detour(side, k, n).wait_recv()
+                    relay(side, k, n).start()
 
     for copy in lists:
         copy.wait()
@@ -229,6 +313,8 @@
         for i in (0, 1):
             wait_recv(kv_copy, kv_routes, i, p)
             start(kv_copy, kv_routes, 4 + i, p)
+        for k in range(len(SEAMS)):
+            pl.when(p == RELAY_AT[k])(lambda: pass_on(k))
         for i in (2, 3):
             wait_recv(kv_copy, kv_routes, i, p)
         tops, sums, parts = weigh(p, EARLY)
@@ -333,6 +419,13 @@
         for i in range(6):
             wait_send(kv_copy, kv_routes, i, p)
             wait_send(t_copy, t_routes, i, p)
+
+    for side, k in sides:
+
+        @pl.when(f == RELAYS[side][k])
+        def _():
+            for n in range(DETOURS[side][k]):
+                relay(side, k, n).wait_send()
 
 
 def hand_over(*refs):
@@ -378,6 +471,12 @@
             pltpu.SemaphoreType.DMA((6, PAIRS)),
             pltpu.SemaphoreType.DMA((6, PAIRS)),
             pltpu.SemaphoreType.DMA((6, PAIRS)),
+            pltpu.VMEM((len(SEAMS), MOST, 2, TOK, PAIR), low),
+            pltpu.SemaphoreType.DMA((len(SEAMS), MOST)),
+            pltpu.SemaphoreType.DMA((len(SEAMS), MOST)),
+            pltpu.SemaphoreType.REGULAR,
+            pltpu.SemaphoreType.REGULAR,
+            pltpu.SemaphoreType.REGULAR,
         ],
         compiler_params=pltpu.CompilerParams(
             collective_id=0, has_side_effects=True, vmem_limit_bytes=48 * 2**20

time: 104 us -> 101 us (0.971)
  Pallas kernels: 101 us -> 98.4 us
    pallas_call x1, Pallas kernels: 100 us -> 97 us  [shards(): pl.pallas_call(kernel, out_shape=(pltpu.VMEM((TOK, WIDTH), low),) * 4, in...]
where the time goes in v3:
time: 101 us; the launch traced here: 99.7 us
  Pallas kernels  98.4 us (97%)
  between operations  1.29 us (1%)
    pallas_call x1, Pallas kernels, shards(): pl.pallas_call(kernel, out_shape=(pltpu.VMEM((TOK, WIDTH), low),) * 4, in...  97 us

profile of v3, /device:TPU:30, one launch (start us, length us, event | category | flops | bytes accessed | tf_op | source)
XLA Modules:
  0.0 99.7 jit_solution(17332560803949754982)
XLA Ops:
  1.3 97.0 %shard_map.93 = (bf16[256,1024]{1,0:T(8,128)(2,1)S(1)}, bf16[256,1024]{1,0:T(8,128)(2,1)S(1)}, bf16[256,1024]{1,0:T(8,128)(2,1)S(1)}, bf16[256,1024]{1,0:T(8,128)(2,1)S(1)}) custom-call(s32[1,6]{1,0:T(1,128)} %partners_hbm.1, s32[1,1]{1,0:T(1,128)} %bitcast.1.counts_hbm, bf16[256,1024]{1,0:T(8,128)(2,1)} %q_hbm.1, bf16[256,1024]{1,0:T(8,128)(2,1)} %k_hbm.1, ...), custom_call_target="tpu_custom_call" | custom-call | tf_op jit(solution)/shard_map/pallas_call | solution.py:446
  98.3 1.3 %shard_map.94 = (bf16[256,1024]{1,0:T(8,128)(2,1)}, bf16[256,1024]{1,0:T(8,128)(2,1)}, bf16[256,1024]{1,0:T(8,128)(2,1)}, bf16[256,1024]{1,0:T(8,128)(2,1)}) custom-call(bf16[256,1024]{1,0:T(8,128)(2,1)S(1)} %get-tuple-element.8.refs_0_, bf16[256,1024]{1,0:T(8,128)(2,1)S(1)} %get-tuple-element.9.refs_1_, bf16[256,1024]{1,0:T(8,128)(2,1)S(1)} %get-tuple-element.10.refs_2_, ...), custom_call_target="tpu_custom_call" | custom-call | tf_op jit(solution)/shard_map/pallas_call | solution.py:489

commit v4 on v3

--- a/solution.py
+++ b/solution.py
@@ -117,18 +117,6 @@
 
         lax.fori_loop(0, PAIRS, step, 0)
 
-    lists = [
-        pltpu.make_async_copy(partners_hbm, partners, list_sem.at[0]),
-        pltpu.make_async_copy(counts_hbm, counts, list_sem.at[1]),
-    ]
-    for copy in lists:
-        copy.start()
-
-    @each_pair
-    def _(p):
-        for i in range(4):
-            fetch(i, p).start()
-
     def signal(semaphore, device):
         pl.semaphore_signal(semaphore, inc=1, device_id=device, device_id_type=MESH)
 
@@ -148,6 +136,11 @@
     signal_frames(f == 16, 23, 8)
     signal_frames(f == 8, 15)
 
+    @each_pair
+    def _(p):
+        for i in (0, 1):
+            fetch(i, p).start()
+
     def amount(condition, count):
         return count * condition.astype(jnp.int32)
 
@@ -170,11 +163,6 @@
         device = (c, SEAMS[k][1 - side])
         return remote(relayed.at[k, n], kv.at[slot, pair], relay_send.at[k, n], kv_recv.at[slot, pair], device)
 
-    @each_pair
-    def _(p):
-        for i in (0, 1):
-            fetch(i, p).wait()
-
     direct = [
         PAIRS - sum(amount(f == seam[side], count) for seam, count in zip(SEAMS, DETOURS[side])) for side in range(2)
     ]
@@ -186,7 +174,13 @@
             kv_copy(i, p).start()
         return carry
 
-    lax.fori_loop(0, HEADSTART, send_own, 0)
+    def fetched(p, carry):
+        for i in (0, 1):
+            fetch(i, p).wait()
+        return carry
+
+    lax.fori_loop(0, HEADSTART, lambda p, carry: send_own(p, fetched(p, carry)), 0)
+    lax.fori_loop(HEADSTART, PAIRS, fetched, 0)
 
     @pl.when(after)
     def _():
@@ -203,6 +197,18 @@
                 detour(side, k, n).start()
 
     lax.fori_loop(HEADSTART, PAIRS, send_own, 0)
+
+    lists = [
+        pltpu.make_async_copy(partners_hbm, partners, list_sem.at[0]),
+        pltpu.make_async_copy(counts_hbm, counts, list_sem.at[1]),
+    ]
+    for copy in lists:
+        copy.start()
+
+    @each_pair
+    def _(p):
+        for i in (2, 3):
+            fetch(i, p).start()
 
     def pass_on(k):
         for side in range(2):
@@ -404,6 +410,20 @@
 
     lax.fori_loop(PAIRS - LAG, PAIRS, flush, 0)
 
+    for side, k in sides:
+
+        @pl.when(f == RELAYS[side][k])
+        def _():
+            for n in range(DETOURS[side][k]):
+                relay(side, k, n).wait_send()
+
+    @each_pair
+    def _(p):
+        for i in range(6):
+            wait_send(kv_copy, kv_routes, i, p)
+        for i in range(4):
+            wait_send(t_copy, t_routes, i, p)
+
     @each_pair
     def _(p):
         for i in range(2, 6):
@@ -413,19 +433,8 @@
             total = total + tin[i, p].astype(jnp.float32)
         dk[:, columns(p)] = total[0].astype(jnp.bfloat16)
         dv[:, columns(p)] = total[1].astype(jnp.bfloat16)
-
-    @each_pair
-    def _(p):
-        for i in range(6):
-            wait_send(kv_copy, kv_routes, i, p)
+        for i in (4, 5):
             wait_send(t_copy, t_routes, i, p)
-
-    for side, k in sides:
-
-        @pl.when(f == RELAYS[side][k])
-        def _():
-            for n in range(DETOURS[side][k]):
-                relay(side, k, n).wait_send()
 
 
 def hand_over(*refs):

time: 101 us -> 101 us (level)
  no operation moved by 1% of the time
where the time goes in v4:
time: 101 us; the launch traced here: 99.3 us
  Pallas kernels  98 us (97%)
  between operations  1.29 us (1%)
    pallas_call x1, Pallas kernels, shards(): pl.pallas_call(kernel, out_shape=(pltpu.VMEM((TOK, WIDTH), low),) * 4, in...  96.6 us

profile of v4, /device:TPU:30, one launch (start us, length us, event | category | flops | bytes accessed | tf_op | source)
XLA Modules:
  0.0 99.3 jit_solution(12247470250992622511)
XLA Ops:
  1.3 96.6 %shard_map.93 = (bf16[256,1024]{1,0:T(8,128)(2,1)S(1)}, bf16[256,1024]{1,0:T(8,128)(2,1)S(1)}, bf16[256,1024]{1,0:T(8,128)(2,1)S(1)}, bf16[256,1024]{1,0:T(8,128)(2,1)S(1)}) custom-call(s32[1,6]{1,0:T(1,128)} %partners_hbm.1, s32[1,1]{1,0:T(1,128)} %bitcast.1.counts_hbm, bf16[256,1024]{1,0:T(8,128)(2,1)} %q_hbm.1, bf16[256,1024]{1,0:T(8,128)(2,1)} %k_hbm.1, ...), custom_call_target="tpu_custom_call" | custom-call | tf_op jit(solution)/shard_map/pallas_call | solution.py:455
  97.9 1.3 %shard_map.94 = (bf16[256,1024]{1,0:T(8,128)(2,1)}, bf16[256,1024]{1,0:T(8,128)(2,1)}, bf16[256,1024]{1,0:T(8,128)(2,1)}, bf16[256,1024]{1,0:T(8,128)(2,1)}) custom-call(bf16[256,1024]{1,0:T(8,128)(2,1)S(1)} %get-tuple-element.8.refs_0_, bf16[256,1024]{1,0:T(8,128)(2,1)S(1)} %get-tuple-element.9.refs_1_, bf16[256,1024]{1,0:T(8,128)(2,1)S(1)} %get-tuple-element.10.refs_2_, ...), custom_call_target="tpu_custom_call" | custom-call | tf_op jit(solution)/shard_map/pallas_call | solution.py:498
